TPU v7x, 256 devices: a whole 4x4x8 slice. The times are simulated.
256 devices in a mesh: expert: 16 (over z, x_lo), tensor: 16 (over x_hi, y, core).
Axes of the slice: x: 4 (x_hi: 2, x_lo: 2; x = x_hi * 2 + x_lo), y: 4, z: 8, core: 2. Of those that a mesh axis runs over, the one named last changes fastest.
Arguments:
- context: bfloat16 [2048, 8192], P('expert', 'tensor'), may hold values from -6 to 6
- proj_weight: bfloat16 [8192, 4096], P('tensor', 'expert'), may hold values from -0.0625 to 0.0625
- norm_gain: float32 [4096], replicated, may hold values from 0.1 to 1.9
- expert_ids: int32 [2048, 8], P(('expert', 'tensor')), may hold values from 0 to 63, all different within a row; in each aligned block of 8 rows (0 to 7, 8 to 15, ...) at most 2 rows name the same one
- gate_values: float32 [2048, 8], P(('expert', 'tensor')), may hold values from 0.1 to 1
- w_gate: bfloat16 [256, 4096, 384], P(('expert', 'tensor')), may hold values from -0.09375 to 0.09375
- w_up: bfloat16 [256, 4096, 384], P(('expert', 'tensor')), may hold values from -0.09375 to 0.09375
- w_down: bfloat16 [256, 384, 4096], P(('expert', 'tensor')), may hold values from -0.15625 to 0.15625
Outputs:
- mixed: bfloat16 [2048, 4096], P(('expert', 'tensor'))
Inputs may be any that keep to these rules, and one draw needn't show every extreme that they name: `expert_ids`: each row names 8 different experts. The tokens fall into aligned blocks of 8 rows, block b holding tokens b * 8 to (b + 1) * 8 - 1; in every block no expert is named by more than 2 rows, a bound that some block reaches.
All inputs are finite; a program needn't handle non-finite values.
Results may differ from a plain program's by a relative error of at most 0.024.
Values may be sent and summed in bfloat16 or wider, within the bound.
No kernel may reach another device: no remote copies, remote signals or barrier semaphores. Data moves between devices by JAX's collectives and lax.ppermute only.
A program may use at most 128 MiB of HBM per device.

v0:
```python
import jax
import jax.numpy as jnp
from jax import lax
from jax.sharding import Mesh
from jax.sharding import PartitionSpec as P

TOPK = 8
QUARTERS = 4
CAP = 2
FINE = ("z", "xl", "xh", "y", "c")
SIZES = (8, 2, 2, 4, 2)
EXPERT = ("z", "xl")
TENSOR = ("xh", "y", "c")
PLANE = ("xh", "y")
NZ = 8


def swap(x, axis):
    return lax.ppermute(x, axis, [(0, 1), (1, 0)])


def fetch(x, hop):
    return lax.ppermute(x, "z", [((i + hop) % NZ, i) for i in range(NZ)])


def gather_z(x):
    up1, dn1 = (fetch(x, 1), fetch(x, -1))
    up2, dn2 = (fetch(x, 2), fetch(x, -2))
    up3, dn3 = (fetch(up1, 2), fetch(dn1, -2))
    far = fetch(up3, 1)
    return [x, up1, up2, up3, far, dn3, dn2, dn1]


def expert_rows(rows, w_gate, w_up, w_down):
    gate_act = jnp.dot(rows, w_gate, preferred_element_type=jnp.float32)
    up_act = jnp.dot(rows, w_up, preferred_element_type=jnp.float32)
    hidden = (jax.nn.silu(gate_act) * up_act).astype(jnp.bfloat16)
    return jnp.dot(hidden, w_down, preferred_element_type=jnp.float32)


def on_device(context, proj_weight, norm_gain, expert_ids, gate_values, w_gate, w_up, w_down):
    zi, xli = (lax.axis_index("z"), lax.axis_index("xl"))
    n_tensor = lax.axis_size(TENSOR)
    n_plane = lax.axis_size(PLANE)
    n_expert = lax.axis_size(EXPERT)
    rows = context.shape[0] // n_tensor
    groups = n_tensor // QUARTERS
    cols = proj_weight.shape[1]
    width = cols * n_expert
    tokens = rows * n_expert
    routing = jnp.concatenate([expert_ids.astype(jnp.float32), gate_values], axis=1)
    routing = lax.all_gather(routing, EXPERT, axis=0, tiled=True)
    other = swap(proj_weight, "xl")
    blocks = [b.reshape(n_tensor, 1, rows, -1) for b in gather_z(context)]
    lhs = jnp.concatenate(blocks, axis=1).reshape(NZ * context.shape[0], -1)
    rhs = jnp.concatenate([proj_weight, other], axis=1)
    partial = jnp.dot(lhs, rhs, preferred_element_type=jnp.float32).astype(jnp.bfloat16)
    partial = partial.reshape(n_tensor, NZ * rows, 2 * cols)
    partial = lax.all_to_all(partial, TENSOR, 0, 0, tiled=True)
    part = jnp.sum(partial.astype(jnp.float32), axis=0).astype(jnp.bfloat16)
    part = jnp.where(xli == 0, part, jnp.concatenate([part[:, cols:], part[:, :cols]], axis=1))
    mate = swap(part, "xl")
    part = part.reshape(NZ, 1, rows, 2 * cols)
    mate = mate.reshape(NZ, 1, rows, 2 * cols)
    pair = jnp.where(
        xli == 0, jnp.concatenate([part, mate], axis=1), jnp.concatenate([mate, part], axis=1)
    )
    start = lax.rem(NZ - zi, NZ)
    pair = lax.dynamic_slice_in_dim(jnp.concatenate([pair, pair], axis=0), start, NZ, axis=0)
    pair = pair.reshape(tokens, 2 * cols)
    attended = jnp.zeros((tokens, width), jnp.bfloat16)
    for hop, block in enumerate(gather_z(pair)):
        at = lax.rem(zi + hop, NZ) * (2 * cols)
        attended = lax.dynamic_update_slice_in_dim(attended, block, at, axis=1)
    stream = attended.astype(jnp.float32)
    scale = lax.rsqrt(jnp.mean(stream * stream, axis=-1, keepdims=True) + 1e-06)
    normed = (stream * scale * norm_gain).astype(jnp.bfloat16)
    ids = routing[:, :TOPK].astype(jnp.int32)
    gates = routing[:, TOPK:]
    ei = zi * 2 + xli
    labels = ei * groups + jnp.arange(groups, dtype=jnp.int32)
    match = ids[:, :, None] == labels[None, None, :]
    chosen = jnp.sum(match.astype(jnp.int32), axis=1)
    weight = jnp.sum(jnp.where(match, gates[:, :, None], 0.0), axis=1)
    blocked = chosen.reshape(n_expert, rows, groups)
    rank = (jnp.cumsum(blocked, axis=1) - blocked).reshape(tokens, groups)
    base = jnp.arange(tokens, dtype=jnp.int32) // rows * CAP
    slot = jnp.where(chosen > 0, base[:, None] + rank, -1)
    slots = n_expert * CAP
    placing = slot[:, :, None] == jnp.arange(slots, dtype=jnp.int32)[None, None, :]
    placing = jnp.repeat(placing, n_plane // groups, axis=1).reshape(tokens, n_plane * slots)
    weight = jnp.repeat(weight, n_plane // groups, axis=1)
    weight = jnp.where(placing, jnp.repeat(weight, slots, axis=1), 0.0)
    sent = lax.dot_general(
        placing.astype(jnp.bfloat16),
        normed,
        (((0,), (0,)), ((), ())),
        preferred_element_type=jnp.float32,
    ).astype(jnp.bfloat16)
    sent = sent.reshape(n_plane, slots, width)
    mine = lax.all_to_all(sent, PLANE, 0, 0, tiled=True).reshape(n_plane * slots, width)
    theirs = swap(mine, "c")
    theirs_out = expert_rows(theirs, w_gate[0], w_up[0], w_down[0]).astype(jnp.bfloat16)
    from_mate = swap(theirs_out, "c")
    mine_out = expert_rows(mine, w_gate[0], w_up[0], w_down[0])
    summed = (mine_out + from_mate.astype(jnp.float32)).astype(jnp.bfloat16)
    summed = summed.reshape(n_plane, slots, width)
    back = lax.all_to_all(summed, PLANE, 0, 0, tiled=True).reshape(n_plane * slots, width)
    high = weight.astype(jnp.bfloat16)
    low = (weight - high.astype(jnp.float32)).astype(jnp.bfloat16)
    mixture = jnp.dot(high, back, preferred_element_type=jnp.float32) + jnp.dot(
        low, back, preferred_element_type=jnp.float32
    )
    mixture = mixture.astype(jnp.bfloat16).reshape(NZ, 2, rows, width)
    keep = lax.dynamic_index_in_dim(mixture, xli, 1, keepdims=False)
    give = lax.dynamic_index_in_dim(mixture, 1 - xli, 1, keepdims=False)
    got = swap(give, "xl")
    half = (keep.astype(jnp.float32) + got.astype(jnp.float32)).astype(jnp.bfloat16)
    home = lax.all_to_all(half, "z", 0, 0, tiled=True)
    own = lax.dynamic_slice_in_dim(attended, ei * rows, rows, axis=0)
    out = own.astype(jnp.float32) + jnp.sum(home.astype(jnp.float32), axis=0)
    return out.astype(jnp.bfloat16)


def solution(mesh):
    fine = Mesh(mesh.devices.reshape(SIZES), FINE)
    both = EXPERT + TENSOR
    return jax.shard_map(
        on_device,
        mesh=fine,
        in_specs=(
            P(EXPERT, TENSOR),
            P(TENSOR, EXPERT),
            P(),
            P(both, None),
            P(both, None),
            P(both, None, None),
            P(both, None, None),
            P(both, None, None),
        ),
        out_specs=P(both, None),
        check_vma=False,
    )
```

profile of v0, /device:TPU:4, one launch (start us, length us, event | category | flops | bytes accessed | tf_op | source)
XLA Modules:
  0.0 236.1 jit_solution(9156243198464693742)
XLA Ops:
  0.0 5.9 %collective-permute-start = (bf16[128,512]{1,0:T(8,128)(2,1)}, bf16[128,512]{1,0:T(8,128)(2,1)S(1)}, u32[]{:S(2)}, u32[]{:S(2)}) collective-permute-start(bf16[128,512]{1,0:T(8,128)(2,1)} %param.8), channel_id=1, source_target_pairs={{32,0},{64,32},{96,64},{128,96},{160,128},{192,160},{224,192},{0,2... | collective-permute-start | bytes 393224 | tf_op jit(solution)/shard_map/ppermute | solution.py:23
  10.9 1.8 collective-permute-done
  12.7 2.0 collective-permute-start.2
  14.7 2.0 collective-permute-done.4
  17.9 1.6 collective-permute-done.2
  19.5 4.2 %collective-permute-start.3 = (bf16[128,512]{1,0:T(8,128)(2,1)S(1)}, bf16[128,512]{1,0:T(8,128)(2,1)S(1)}, u32[]{:S(2)}, u32[]{:S(2)}) collective-permute-start(bf16[128,512]{1,0:T(8,128)(2,1)S(1)} %collective-permute-done.2), channel_id=1, source_target_pairs={{32,0},{64,32},{96,64},{128,96},{160,128},{192,160},{224,192},{0,2... | collective-permute-start | bytes 393224 | tf_op jit(solution)/shard_map/ppermute | solution.py:23
  23.7 2.5 %collective-permute-done.3 = bf16[128,512]{1,0:T(8,128)(2,1)S(1)} collective-permute-done((bf16[128,512]{1,0:T(8,128)(2,1)S(1)}, bf16[128,512]{1,0:T(8,128)(2,1)S(1)}, u32[]{:S(2)}, u32[]{:S(2)}) %collective-permute-start.3) | collective-permute-done | bytes 131104 | tf_op jit(solution)/shard_map/ppermute | solution.py:23
  26.4 1.7 convolution_convert_fusion.2
  28.1 7.4 %all-to-all-start = ((bf16[16,64,512]{2,1,0:T(8,128)(2,1)}), bf16[16,64,512]{2,1,0:T(8,128)(2,1)}, u32[]{:S(2)}, u32[]{:S(2)}) async-start(bf16[16,64,512]{2,1,0:T(8,128)(2,1)} %bitcast.87), calls=%async_computation | async-start | bytes 2097152 | tf_op jit(solution)/shard_map/all_to_all | solution.py:59
  35.6 41.1 %all_gather.3 = f32[128,16]{1,0:T(8,128)S(1)} all-gather(f32[8,16]{1,0:T(8,128)S(1)} %pad_maximum_fusion), channel_id=1, replica_groups=mesh['z'=8,'xl'=2,'xh'=2,'y'=4,'c'=2] {'z','xl'}, dimensions={0}, use_global_device_ids=true | all-gather | bytes 8704 | tf_op jit(solution)/shard_map/all_gather | solution.py:52
  79.4 4.2 %collective-permute-done.8 = bf16[64,512]{1,0:T(8,128)(2,1)S(1)} collective-permute-done((bf16[64,512]{1,0:T(8,128)(2,1)S(1)}, bf16[64,512]{1,0:T(8,128)(2,1)S(1)}, u32[]{:S(2)}, u32[]{:S(2)}) %collective-permute-start.8) | collective-permute-done | bytes 65568 | tf_op jit(solution)/shard_map/ppermute | solution.py:19
  83.8 2.0 collective-permute-start.13
  86.0 2.9 %collective-permute-start.15 = (bf16[128,512]{1,0:T(8,128)(2,1)S(1)}, bf16[128,512]{1,0:T(8,128)(2,1)S(1)}, u32[]{:S(2)}, u32[]{:S(2)}) collective-permute-start(bf16[128,512]{1,0:T(8,128)(2,1)S(1)} %bitcast.91), channel_id=1, source_target_pairs={{192,0},{224,32},{0,64},{32,96},{64,128},{96,160},{128,192},{160,2... | collective-permute-start | bytes 393224 | tf_op jit(solution)/shard_map/ppermute | solution.py:23
  90.6 1.6 collective-permute-done.13
  93.5 3.5 %collective-permute-done.11 = bf16[128,512]{1,0:T(8,128)(2,1)S(1)} collective-permute-done((bf16[128,512]{1,0:T(8,128)(2,1)}, bf16[128,512]{1,0:T(8,128)(2,1)S(1)}, u32[]{:S(2)}, u32[]{:S(2)}) %collective-permute-start.11) | collective-permute-done | bytes 131104 | tf_op jit(solution)/shard_map/ppermute | solution.py:23
  97.0 3.2 %collective-permute-start.12 = (bf16[128,512]{1,0:T(8,128)(2,1)S(1)}, bf16[128,512]{1,0:T(8,128)(2,1)S(1)}, u32[]{:S(2)}, u32[]{:S(2)}) collective-permute-start(bf16[128,512]{1,0:T(8,128)(2,1)S(1)} %collective-permute-done.11), channel_id=1, source_target_pairs={{32,0},{64,32},{96,64},{128,96},{160,128},{192,160},{224,192},{0,2... | collective-permute-start | bytes 393224 | tf_op jit(solution)/shard_map/ppermute | solution.py:23
  100.2 2.5 %collective-permute-done.12 = bf16[128,512]{1,0:T(8,128)(2,1)S(1)} collective-permute-done((bf16[128,512]{1,0:T(8,128)(2,1)S(1)}, bf16[128,512]{1,0:T(8,128)(2,1)S(1)}, u32[]{:S(2)}, u32[]{:S(2)}) %collective-permute-start.12) | collective-permute-done | bytes 131104 | tf_op jit(solution)/shard_map/ppermute | solution.py:23
  103.9 24.9 %all_to_all.20 = bf16[8,32,4096]{2,1,0:T(8,128)(2,1)S(1)} all-to-all(bf16[8,32,4096]{2,1,0:T(8,128)(2,1)S(1)} %bitcast.80), channel_id=1, replica_groups=mesh['z'=8,'xl'=2,'xh'=2,'y'=4,'c'=2] {'xh','y'}, dimensions={0} | all-to-all | bytes 4194304 | tf_op jit(solution)/shard_map/all_to_all | solution.py:101
  130.1 4.2 %collective-permute-done.16 = bf16[256,4096]{1,0:T(8,128)(2,1)S(1)} collective-permute-done((bf16[256,4096]{1,0:T(8,128)(2,1)S(1)}, bf16[256,4096]{1,0:T(8,128)(2,1)S(1)}, u32[]{:S(2)}, u32[]{:S(2)}) %collective-permute-start.16) | collective-permute-done | bytes 2097184 | tf_op jit(solution)/shard_map/ppermute | solution.py:19
  135.7 2.1 fusion.6
  137.7 6.4 %convolution_convert_fusion.1 = bf16[256,4096]{1,0:T(8,128)(2,1)} fusion(bf16[1,384,4096]{2,1,0:T(8,128)(2,1)S(1)} %copy-done, f32[256,384]{1,0:T(8,128)} %fusion.6, bf16[256,4096]{1,0:T(8,128)(2,1)} %copy-done.8, bf16[1,4096,384]{2,1,0:T(8,128)(2,1)} %param.13), kind=kOutput, calls=%fused_computation.1 | convolution fusion | flops 1612251136 | bytes 10878976 | tf_op jit(solution)/shard_map/dot_general | solution.py:38
  144.2 4.5 %fusion.12 = f32[256,384]{1,0:T(8,128)} fusion(bf16[256,4096]{1,0:T(8,128)(2,1)} %bitcast.85, bf16[1,4096,384]{2,1,0:T(8,128)(2,1)} %param.13), kind=kOutput, calls=%fused_computation.14 | convolution fusion | flops 805306368 | bytes 5636096 | tf_op jit(solution)/shard_map/dot_general | solution.py:35
  148.8 7.0 %add_convert_fusion = bf16[256,4096]{1,0:T(8,128)(2,1)} fusion(bf16[256,4096]{1,0:T(8,128)(2,1)} %collective-permute-done.17, bf16[1,384,4096]{2,1,0:T(8,128)(2,1)S(1)} %copy-done, bf16[256,4096]{1,0:T(8,128)(2,1)} %bitcast.86, bf16[1,4096,384]{2,1,0:T(8,128)(2,1)} %param.14, f32[256,384]{1,0:T(8,128)} %fusion.12), kind=kOutput, calls=%fused_computation.4 | convolution fusion | flops 1614348288 | bytes 12976128 | tf_op jit(solution)/shard_map/dot_general | solution.py:38
  155.8 7.2 %all-to-all-start.2 = ((bf16[8,32,4096]{2,1,0:T(8,128)(2,1)}), bf16[8,32,4096]{2,1,0:T(8,128)(2,1)}, u32[]{:S(2)}, u32[]{:S(2)}) async-start(bf16[8,32,4096]{2,1,0:T(8,128)(2,1)} %bitcast.83), calls=%async_computation.2 | async-start | bytes 4194304 | tf_op jit(solution)/shard_map/all_to_all | solution.py:108
  163.2 26.2 %all-to-all-done.2 = bf16[8,32,4096]{2,1,0:T(8,128)(2,1)} async-done(((bf16[8,32,4096]{2,1,0:T(8,128)(2,1)}), bf16[8,32,4096]{2,1,0:T(8,128)(2,1)}, u32[]{:S(2)}, u32[]{:S(2)}) %all-to-all-start.2) | async-done | bytes 2097184 | tf_op jit(solution)/shard_map/all_to_all | solution.py:108
  189.4 2.1 fusion.52
  191.4 2.1 fusion
  195.4 13.9 %collective-permute-done.18 = bf16[8,8,4096]{2,1,0:T(8,128)(2,1)} collective-permute-done((bf16[8,8,4096]{2,1,0:T(8,128)(2,1)}, bf16[8,8,4096]{2,1,0:T(8,128)(2,1)}, u32[]{:S(2)}, u32[]{:S(2)}) %collective-permute-start.18) | collective-permute-done | bytes 524320 | tf_op jit(solution)/shard_map/ppermute | solution.py:19
  209.3 2.1 fusion.24
  211.5 5.4 %all-to-all-start.3 = ((bf16[8,8,4096]{2,1,0:T(8,128)(2,1)}), bf16[8,8,4096]{2,1,0:T(8,128)(2,1)}, u32[]{:S(2)}, u32[]{:S(2)}) async-start(bf16[8,8,4096]{2,1,0:T(8,128)(2,1)} %fusion.24), calls=%async_computation.3 | async-start | bytes 1048576 | tf_op jit(solution)/shard_map/all_to_all | solution.py:119
  216.9 16.7 %all-to-all-done.3 = bf16[8,8,4096]{2,1,0:T(8,128)(2,1)} async-done(((bf16[8,8,4096]{2,1,0:T(8,128)(2,1)}), bf16[8,8,4096]{2,1,0:T(8,128)(2,1)}, u32[]{:S(2)}, u32[]{:S(2)}) %all-to-all-start.3) | async-done | bytes 524320 | tf_op jit(solution)/shard_map/all_to_all | solution.py:119
  234.6 1.5 add_convert_fusion.1
  (89 shorter events, 19.3 us)
Async XLA Ops:
  0.0 137.7 %copy-start = (bf16[1,384,4096]{2,1,0:T(8,128)(2,1)S(1)}, bf16[1,384,4096]{2,1,0:T(8,128)(2,1)}, u32[]{:S(2)}) copy-start(bf16[1,384,4096]{2,1,0:T(8,128)(2,1)} %param.15) | copy-start | bytes 9437188
  0.0 26.3 %copy-start.9 = (bf16[512,256]{1,0:T(8,128)(2,1)S(1)}, bf16[512,256]{1,0:T(8,128)(2,1)}, u32[]{:S(2)}) copy-start(bf16[512,256]{1,0:T(8,128)(2,1)} %param.9) | copy-start | bytes 786436
  0.0 12.7 %collective-permute-start = (bf16[128,512]{1,0:T(8,128)(2,1)}, bf16[128,512]{1,0:T(8,128)(2,1)S(1)}, u32[]{:S(2)}, u32[]{:S(2)}) collective-permute-start(bf16[128,512]{1,0:T(8,128)(2,1)} %param.8), channel_id=1, source_target_pairs={{32,0},{64,32},{96,64},{128,96},{160,128},{192,160},{224,192},{0,2... | collective-permute-start | bytes 393224 | tf_op jit(solution)/shard_map/ppermute | solution.py:23
  5.9 12.0 %collective-permute-start.1 = (bf16[128,512]{1,0:T(8,128)(2,1)}, bf16[128,512]{1,0:T(8,128)(2,1)S(1)}, u32[]{:S(2)}, u32[]{:S(2)}) collective-permute-start(bf16[128,512]{1,0:T(8,128)(2,1)} %param.8), channel_id=1, source_target_pairs={{64,0},{96,32},{128,64},{160,96},{192,128},{224,160},{0,192},{32,2... | collective-permute-start | bytes 393224 | tf_op jit(solution)/shard_map/ppermute | solution.py:23
  7.3 9.4 %collective-permute-start.4 = (bf16[128,512]{1,0:T(8,128)(2,1)}, bf16[128,512]{1,0:T(8,128)(2,1)S(1)}, u32[]{:S(2)}, u32[]{:S(2)}) collective-permute-start(bf16[128,512]{1,0:T(8,128)(2,1)} %param.8), channel_id=1, source_target_pairs={{224,0},{0,32},{32,64},{64,96},{96,128},{128,160},{160,192},{192,2... | collective-permute-start | bytes 393224 | tf_op jit(solution)/shard_map/ppermute | solution.py:23
  8.3 17.9 %collective-permute-start.6 = (bf16[128,512]{1,0:T(8,128)(2,1)}, bf16[128,512]{1,0:T(8,128)(2,1)S(1)}, u32[]{:S(2)}, u32[]{:S(2)}) collective-permute-start(bf16[128,512]{1,0:T(8,128)(2,1)} %param.8), channel_id=1, source_target_pairs={{192,0},{224,32},{0,64},{32,96},{64,128},{96,160},{128,192},{160,2... | collective-permute-start | bytes 393224 | tf_op jit(solution)/shard_map/ppermute | solution.py:23
  8.8 17.5 %collective-permute-start.7 = (bf16[512,256]{1,0:T(8,128)(2,1)}, bf16[512,256]{1,0:T(8,128)(2,1)S(1)}, u32[]{:S(2)}, u32[]{:S(2)}) collective-permute-start(bf16[512,256]{1,0:T(8,128)(2,1)} %param.9), channel_id=1, source_target_pairs={{0,16},{16,0},{1,17},{17,1},{2,18},{18,2},{3,19},{19,3},{4,20},{20... | collective-permute-start | bytes 786440 | tf_op jit(solution)/shard_map/ppermute | solution.py:19
  12.7 6.9 %collective-permute-start.2 = (bf16[128,512]{1,0:T(8,128)(2,1)S(1)}, bf16[128,512]{1,0:T(8,128)(2,1)S(1)}, u32[]{:S(2)}, u32[]{:S(2)}) collective-permute-start(bf16[128,512]{1,0:T(8,128)(2,1)S(1)} %collective-permute-done), channel_id=1, source_target_pairs={{64,0},{96,32},{128,64},{160,96},{192,128},{224,160},{0,192},{32,2... | collective-permute-start | bytes 393224 | tf_op jit(solution)/shard_map/ppermute | solution.py:23
  16.7 9.5 %collective-permute-start.5 = (bf16[128,512]{1,0:T(8,128)(2,1)S(1)}, bf16[128,512]{1,0:T(8,128)(2,1)S(1)}, u32[]{:S(2)}, u32[]{:S(2)}) collective-permute-start(bf16[128,512]{1,0:T(8,128)(2,1)S(1)} %collective-permute-done.4), channel_id=1, source_target_pairs={{192,0},{224,32},{0,64},{32,96},{64,128},{96,160},{128,192},{160,2... | collective-permute-start | bytes 393224 | tf_op jit(solution)/shard_map/ppermute | solution.py:23
  19.5 6.7 %collective-permute-start.3 = (bf16[128,512]{1,0:T(8,128)(2,1)S(1)}, bf16[128,512]{1,0:T(8,128)(2,1)S(1)}, u32[]{:S(2)}, u32[]{:S(2)}) collective-permute-start(bf16[128,512]{1,0:T(8,128)(2,1)S(1)} %collective-permute-done.2), channel_id=1, source_target_pairs={{32,0},{64,32},{96,64},{128,96},{160,128},{192,160},{224,192},{0,2... | collective-permute-start | bytes 393224 | tf_op jit(solution)/shard_map/ppermute | solution.py:23
  26.3 9.2 %copy-start.6 = (s32[8,8]{1,0:T(8,128)S(1)}, s32[8,8]{1,0:T(8,128)}, u32[]{:S(2)}) copy-start(s32[8,8]{1,0:T(8,128)} %param.11) | copy-start | bytes 772
  26.4 9.2 %copy-start.5 = (f32[8,8]{1,0:T(8,128)S(1)}, f32[8,8]{1,0:T(8,128)}, u32[]{:S(2)}) copy-start(f32[8,8]{1,0:T(8,128)} %param.12) | copy-start | bytes 772
  28.1 49.8 %all-to-all-start = ((bf16[16,64,512]{2,1,0:T(8,128)(2,1)}), bf16[16,64,512]{2,1,0:T(8,128)(2,1)}, u32[]{:S(2)}, u32[]{:S(2)}) async-start(bf16[16,64,512]{2,1,0:T(8,128)(2,1)} %bitcast.87), calls=%async_computation | async-start | bytes 2097152 | tf_op jit(solution)/shard_map/all_to_all | solution.py:59
  79.3 4.4 %collective-permute-start.8 = (bf16[64,512]{1,0:T(8,128)(2,1)S(1)}, bf16[64,512]{1,0:T(8,128)(2,1)S(1)}, u32[]{:S(2)}, u32[]{:S(2)}) collective-permute-start(bf16[64,512]{1,0:T(8,128)(2,1)S(1)} %maximum_select_fusion.2), channel_id=1, source_target_pairs={{0,16},{16,0},{1,17},{17,1},{2,18},{18,2},{3,19},{19,3},{4,20},{20... | collective-permute-start | bytes 196616 | tf_op jit(solution)/shard_map/ppermute | solution.py:19
  83.8 5.5 %collective-permute-start.9 = (bf16[128,512]{1,0:T(8,128)(2,1)S(1)}, bf16[128,512]{1,0:T(8,128)(2,1)}, u32[]{:S(2)}, u32[]{:S(2)}) collective-permute-start(bf16[128,512]{1,0:T(8,128)(2,1)S(1)} %bitcast.88), channel_id=1, source_target_pairs={{32,0},{64,32},{96,64},{128,96},{160,128},{192,160},{224,192},{0,2... | collective-permute-start | bytes 393224 | tf_op jit(solution)/shard_map/ppermute | solution.py:23
  83.8 8.4 %collective-permute-start.13 = (bf16[128,512]{1,0:T(8,128)(2,1)S(1)}, bf16[128,512]{1,0:T(8,128)(2,1)S(1)}, u32[]{:S(2)}, u32[]{:S(2)}) collective-permute-start(bf16[128,512]{1,0:T(8,128)(2,1)S(1)} %bitcast.89), channel_id=1, source_target_pairs={{224,0},{0,32},{32,64},{64,96},{96,128},{128,160},{160,192},{192,2... | collective-permute-start | bytes 393224 | tf_op jit(solution)/shard_map/ppermute | solution.py:23
  85.9 17.2 %copy-start.4 = (f32[4096]{0:T(1024)S(1)}, f32[4096]{0:T(1024)}, u32[]{:S(2)}) copy-start(f32[4096]{0:T(1024)} %param.10) | copy-start | bytes 49156
  85.9 14.2 %collective-permute-start.10 = (bf16[128,512]{1,0:T(8,128)(2,1)S(1)}, bf16[128,512]{1,0:T(8,128)(2,1)S(1)}, u32[]{:S(2)}, u32[]{:S(2)}) collective-permute-start(bf16[128,512]{1,0:T(8,128)(2,1)S(1)} %bitcast.90), channel_id=1, source_target_pairs={{64,0},{96,32},{128,64},{160,96},{192,128},{224,160},{0,192},{32,2... | collective-permute-start | bytes 393224 | tf_op jit(solution)/shard_map/ppermute | solution.py:23
  86.0 16.7 %collective-permute-start.15 = (bf16[128,512]{1,0:T(8,128)(2,1)S(1)}, bf16[128,512]{1,0:T(8,128)(2,1)S(1)}, u32[]{:S(2)}, u32[]{:S(2)}) collective-permute-start(bf16[128,512]{1,0:T(8,128)(2,1)S(1)} %bitcast.91), channel_id=1, source_target_pairs={{192,0},{224,32},{0,64},{32,96},{64,128},{96,160},{128,192},{160,2... | collective-permute-start | bytes 393224 | tf_op jit(solution)/shard_map/ppermute | solution.py:23
  89.2 7.7 %collective-permute-start.11 = (bf16[128,512]{1,0:T(8,128)(2,1)}, bf16[128,512]{1,0:T(8,128)(2,1)S(1)}, u32[]{:S(2)}, u32[]{:S(2)}) collective-permute-start(bf16[128,512]{1,0:T(8,128)(2,1)} %collective-permute-done.9), channel_id=1, source_target_pairs={{64,0},{96,32},{128,64},{160,96},{192,128},{224,160},{0,192},{32,2... | collective-permute-start | bytes 393224 | tf_op jit(solution)/shard_map/ppermute | solution.py:23
  92.2 10.5 %collective-permute-start.14 = (bf16[128,512]{1,0:T(8,128)(2,1)S(1)}, bf16[128,512]{1,0:T(8,128)(2,1)S(1)}, u32[]{:S(2)}, u32[]{:S(2)}) collective-permute-start(bf16[128,512]{1,0:T(8,128)(2,1)S(1)} %collective-permute-done.13), channel_id=1, source_target_pairs={{192,0},{224,32},{0,64},{32,96},{64,128},{96,160},{128,192},{160,2... | collective-permute-start | bytes 393224 | tf_op jit(solution)/shard_map/ppermute | solution.py:23
  97.0 5.7 %collective-permute-start.12 = (bf16[128,512]{1,0:T(8,128)(2,1)S(1)}, bf16[128,512]{1,0:T(8,128)(2,1)S(1)}, u32[]{:S(2)}, u32[]{:S(2)}) collective-permute-start(bf16[128,512]{1,0:T(8,128)(2,1)S(1)} %collective-permute-done.11), channel_id=1, source_target_pairs={{32,0},{64,32},{96,64},{128,96},{160,128},{192,160},{224,192},{0,2... | collective-permute-start | bytes 393224 | tf_op jit(solution)/shard_map/ppermute | solution.py:23
  102.8 1.1 copy-start.1
  103.9 31.8 %copy-start.7 = (bf16[1,4096,384]{2,1,0:T(8,128)(2,1)S(1)}, bf16[1,4096,384]{2,1,0:T(8,128)(2,1)}, u32[]{:S(2)}) copy-start(bf16[1,4096,384]{2,1,0:T(8,128)(2,1)} %param.14) | copy-start | bytes 9437188
  128.8 1.3 copy-start.3
  130.1 4.2 %collective-permute-start.16 = (bf16[256,4096]{1,0:T(8,128)(2,1)S(1)}, bf16[256,4096]{1,0:T(8,128)(2,1)S(1)}, u32[]{:S(2)}, u32[]{:S(2)}) collective-permute-start(bf16[256,4096]{1,0:T(8,128)(2,1)S(1)} %bitcast.84), channel_id=1, source_target_pairs={{0,1},{1,0},{2,3},{3,2},{4,5},{5,4},{6,7},{7,6},{8,9},{9,8},{10,11... | collective-permute-start | bytes 6291464 | tf_op jit(solution)/shard_map/ppermute | solution.py:19
  134.3 1.4 copy-start.8
  144.1 4.7 %collective-permute-start.17 = (bf16[256,4096]{1,0:T(8,128)(2,1)}, bf16[256,4096]{1,0:T(8,128)(2,1)}, u32[]{:S(2)}, u32[]{:S(2)}) collective-permute-start(bf16[256,4096]{1,0:T(8,128)(2,1)} %convolution_convert_fusion.1), channel_id=1, source_target_pairs={{0,1},{1,0},{2,3},{3,2},{4,5},{5,4},{6,7},{7,6},{8,9},{9,8},{10,11... | collective-permute-start | bytes 6291464 | tf_op jit(solution)/shard_map/ppermute | solution.py:19
  155.8 33.6 %all-to-all-start.2 = ((bf16[8,32,4096]{2,1,0:T(8,128)(2,1)}), bf16[8,32,4096]{2,1,0:T(8,128)(2,1)}, u32[]{:S(2)}, u32[]{:S(2)}) async-start(bf16[8,32,4096]{2,1,0:T(8,128)(2,1)} %bitcast.83), calls=%async_computation.2 | async-start | bytes 4194304 | tf_op jit(solution)/shard_map/all_to_all | solution.py:108
  193.6 1.0 copy-start.2
  195.4 13.9 %collective-permute-start.18 = (bf16[8,8,4096]{2,1,0:T(8,128)(2,1)}, bf16[8,8,4096]{2,1,0:T(8,128)(2,1)}, u32[]{:S(2)}, u32[]{:S(2)}) collective-permute-start(bf16[8,8,4096]{2,1,0:T(8,128)(2,1)} %dynamic-slice_bitcast_fusion), channel_id=1, source_target_pairs={{0,16},{16,0},{1,17},{17,1},{2,18},{18,2},{3,19},{19,3},{4,20},{20... | collective-permute-start | bytes 1572872 | tf_op jit(solution)/shard_map/ppermute | solution.py:19
  211.5 22.0 %all-to-all-start.3 = ((bf16[8,8,4096]{2,1,0:T(8,128)(2,1)}), bf16[8,8,4096]{2,1,0:T(8,128)(2,1)}, u32[]{:S(2)}, u32[]{:S(2)}) async-start(bf16[8,8,4096]{2,1,0:T(8,128)(2,1)} %fusion.24), calls=%async_computation.3 | async-start | bytes 1048576 | tf_op jit(solution)/shard_map/all_to_all | solution.py:119
where the time goes:
time: 237 us; the launch traced here: 236 us
  waiting for transfers between devices  81.1 us (34%)
  blocking collectives  66 us (28%)
  starting transfers between devices  47.3 us (20%)
  matrix products  26.7 us (11%)
  other arithmetic  7.58 us (3%)
  local copies, waits for them, and re-layouts  7.07 us (3%)
    all_gather x1, blocking collectives, on_device(): routing = lax.all_gather(routing, EXPERT, axis=0, tiled=True)  41.1 us
    all_to_all x1, waiting for transfers between devices, on_device(): lax.all_to_all(summed, PLANE, 0, 0, tiled=True)  26.2 us
    ppermute x14, starting transfers between devices, fetch(): return lax.ppermute(x, 'z', [((i + hop) % NZ, i) for i in range(NZ)])  25.9 us
    all_to_all x1, blocking collectives, on_device(): lax.all_to_all(sent, PLANE, 0, 0, tiled=True)  24.9 us
    ppermute x5, waiting for transfers between devices, swap(): return lax.ppermute(x, axis, [(0, 1), (1, 0)])  22.3 us
    all_to_all x1, waiting for transfers between devices, on_device(): home = lax.all_to_all(half, 'z', 0, 0, tiled=True)  16.7 us
    ppermute x14, waiting for transfers between devices, fetch(): return lax.ppermute(x, 'z', [((i + hop) % NZ, i) for i in range(NZ)])  15.9 us
    dot_general x2, matrix products, expert_rows(): return jnp.dot(hidden, w_down, preferred_element_type=jnp.float32)  13.4 us
  transfers between devices with their start and end apart: 22, of which 13 were waited for; matrix products, arithmetic and copies ran while one was open for 3% of the time, Pallas kernels for 0%

commit v1 on v0

--- a/solution.py
+++ b/solution.py
@@ -49,7 +49,9 @@
     width = cols * n_expert
     tokens = rows * n_expert
     routing = jnp.concatenate([expert_ids.astype(jnp.float32), gate_values], axis=1)
-    routing = lax.all_gather(routing, EXPERT, axis=0, tiled=True)
+    routing = jnp.concatenate(
+        lax.all_to_all(jnp.stack([routing] * lax.axis_size(EXPERT)), EXPERT, 0, 0), axis=0
+    )
     other = swap(proj_weight, "xl")
     blocks = [b.reshape(n_tensor, 1, rows, -1) for b in gather_z(context)]
     lhs = jnp.concatenate(blocks, axis=1).reshape(NZ * context.shape[0], -1)

time: 237 us -> 228 us (0.962)
  blocking collectives: 66 us -> 30 us
  starting transfers between devices: 47.3 us -> 58.8 us
  waiting for transfers between devices: 81.1 us -> 92.2 us
    all_gather x1 -> x0, blocking collectives: 41.1 us -> none  [on_device(): routing = lax.all_gather(routing, EXPERT, axis=0, tiled=True)]
    all_to_all x1, waiting for transfers between devices: 0.01 us -> 12.9 us  [on_device(): partial = lax.all_to_all(partial, TENSOR, 0, 0, tiled=True)]
    all_to_all x0 -> x1, starting transfers between devices: none -> 6.14 us  [on_device(): lax.all_to_all(jnp.stack([routing] * lax.axis_size(EXPERT)), EXPERT, 0, 0)]
    all_to_all x1, blocking collectives: 24.9 us -> 30 us  [on_device(): lax.all_to_all(sent, PLANE, 0, 0, tiled=True)]
    unnamed x28 -> x26, local copies, waits for them, and re-layouts: 4.73 us -> 7.31 us
  transfers between devices with their start and end apart: 22 -> 23, of which waited for: 13 -> 12; matrix products, arithmetic and copies ran while one was open for 3% -> 6% of each run, Pallas kernels for 0% -> 0%
where the time goes in v1:
time: 228 us; the launch traced here: 227 us
  waiting for transfers between devices  92.2 us (40%)
  starting transfers between devices  58.8 us (26%)
  blocking collectives  30 us (13%)
  matrix products  26.7 us (12%)
  other arithmetic  9.6 us (4%)
  local copies, waits for them, and re-layouts  9.27 us (4%)
    all_to_all x1, blocking collectives, on_device(): lax.all_to_all(sent, PLANE, 0, 0, tiled=True)  30 us
    ppermute x14, starting transfers between devices, fetch(): return lax.ppermute(x, 'z', [((i + hop) % NZ, i) for i in range(NZ)])  27 us
    all_to_all x1, waiting for transfers between devices, on_device(): lax.all_to_all(summed, PLANE, 0, 0, tiled=True)  26.2 us
    ppermute x5, waiting for transfers between devices, swap(): return lax.ppermute(x, axis, [(0, 1), (1, 0)])  20.8 us
    all_to_all x1, waiting for transfers between devices, on_device(): home = lax.all_to_all(half, 'z', 0, 0, tiled=True)  17 us
    ppermute x14, waiting for transfers between devices, fetch(): return lax.ppermute(x, 'z', [((i + hop) % NZ, i) for i in range(NZ)])  15.2 us
    dot_general x2, matrix products, expert_rows(): return jnp.dot(hidden, w_down, preferred_element_type=jnp.float32)  13.4 us
    all_to_all x1, waiting for transfers between devices, on_device(): partial = lax.all_to_all(partial, TENSOR, 0, 0, tiled=True)  12.9 us
  transfers between devices with their start and end apart: 23, of which 12 were waited for; matrix products, arithmetic and copies ran while one was open for 6% of the time, Pallas kernels for 0%

profile of v1, /device:TPU:4, one launch (start us, length us, event | category | flops | bytes accessed | tf_op | source)
XLA Modules:
  0.0 226.9 jit_solution(14166903471669884197)
XLA Ops:
  0.0 5.9 %collective-permute-start = (bf16[128,512]{1,0:T(8,128)(2,1)}, bf16[128,512]{1,0:T(8,128)(2,1)}, u32[]{:S(2)}, u32[]{:S(2)}) collective-permute-start(bf16[128,512]{1,0:T(8,128)(2,1)} %param.8), channel_id=1, source_target_pairs={{32,0},{64,32},{96,64},{128,96},{160,128},{192,160},{224,192},{0,2... | collective-permute-start | bytes 393224 | tf_op jit(solution)/shard_map/ppermute | solution.py:23
  10.9 6.1 %all-to-all-start.1 = ((f32[16,1,128]{2,1,0:T(1,128)}), f32[16,1,128]{2,1,0:T(1,128)S(1)}, u32[]{:S(2)}, u32[]{:S(2)}) async-start(f32[16,1,128]{2,1,0:T(1,128)} %reshape.201), calls=%async_computation.1 | async-start | bytes 16384 | tf_op jit(solution)/shard_map/all_to_all | solution.py:53
  17.1 2.0 collective-permute-start.7
  20.0 3.7 %collective-permute-start.2 = (bf16[128,512]{1,0:T(8,128)(2,1)}, bf16[128,512]{1,0:T(8,128)(2,1)S(1)}, u32[]{:S(2)}, u32[]{:S(2)}) collective-permute-start(bf16[128,512]{1,0:T(8,128)(2,1)} %collective-permute-done), channel_id=1, source_target_pairs={{64,0},{96,32},{128,64},{160,96},{192,128},{224,160},{0,192},{32,2... | collective-permute-start | bytes 393224 | tf_op jit(solution)/shard_map/ppermute | solution.py:23
  25.6 2.4 %collective-permute-done.2 = bf16[128,512]{1,0:T(8,128)(2,1)S(1)} collective-permute-done((bf16[128,512]{1,0:T(8,128)(2,1)}, bf16[128,512]{1,0:T(8,128)(2,1)S(1)}, u32[]{:S(2)}, u32[]{:S(2)}) %collective-permute-start.2) | collective-permute-done | bytes 131104 | tf_op jit(solution)/shard_map/ppermute | solution.py:23
  27.9 2.7 %collective-permute-start.3 = (bf16[128,512]{1,0:T(8,128)(2,1)S(1)}, bf16[128,512]{1,0:T(8,128)(2,1)S(1)}, u32[]{:S(2)}, u32[]{:S(2)}) collective-permute-start(bf16[128,512]{1,0:T(8,128)(2,1)S(1)} %collective-permute-done.2), channel_id=1, source_target_pairs={{32,0},{64,32},{96,64},{128,96},{160,128},{192,160},{224,192},{0,2... | collective-permute-start | bytes 393224 | tf_op jit(solution)/shard_map/ppermute | solution.py:23
  30.7 2.5 %collective-permute-done.3 = bf16[128,512]{1,0:T(8,128)(2,1)S(1)} collective-permute-done((bf16[128,512]{1,0:T(8,128)(2,1)S(1)}, bf16[128,512]{1,0:T(8,128)(2,1)S(1)}, u32[]{:S(2)}, u32[]{:S(2)}) %collective-permute-start.3) | collective-permute-done | bytes 131104 | tf_op jit(solution)/shard_map/ppermute | solution.py:23
  33.3 1.7 convolution_convert_fusion.2
  35.0 7.4 %all-to-all-start = ((bf16[16,64,512]{2,1,0:T(8,128)(2,1)}), bf16[16,64,512]{2,1,0:T(8,128)(2,1)}, u32[]{:S(2)}, u32[]{:S(2)}) async-start(bf16[16,64,512]{2,1,0:T(8,128)(2,1)} %bitcast.88), calls=%async_computation | async-start | bytes 2097152 | tf_op jit(solution)/shard_map/all_to_all | solution.py:61
  44.9 12.9 %all-to-all-done = bf16[16,64,512]{2,1,0:T(8,128)(2,1)} async-done(((bf16[16,64,512]{2,1,0:T(8,128)(2,1)}), bf16[16,64,512]{2,1,0:T(8,128)(2,1)}, u32[]{:S(2)}, u32[]{:S(2)}) %all-to-all-start) | async-done | bytes 1048608 | tf_op jit(solution)/shard_map/all_to_all | solution.py:61
  59.4 4.1 %collective-permute-done.8 = bf16[64,512]{1,0:T(8,128)(2,1)S(1)} collective-permute-done((bf16[64,512]{1,0:T(8,128)(2,1)S(1)}, bf16[64,512]{1,0:T(8,128)(2,1)S(1)}, u32[]{:S(2)}, u32[]{:S(2)}) %collective-permute-start.8) | collective-permute-done | bytes 65568 | tf_op jit(solution)/shard_map/ppermute | solution.py:19
  63.7 3.7 %collective-permute-start.9 = (bf16[128,512]{1,0:T(8,128)(2,1)S(1)}, bf16[128,512]{1,0:T(8,128)(2,1)S(1)}, u32[]{:S(2)}, u32[]{:S(2)}) collective-permute-start(bf16[128,512]{1,0:T(8,128)(2,1)S(1)} %bitcast.90), channel_id=1, source_target_pairs={{32,0},{64,32},{96,64},{128,96},{160,128},{192,160},{224,192},{0,2... | collective-permute-start | bytes 393224 | tf_op jit(solution)/shard_map/ppermute | solution.py:23
  67.4 2.7 %collective-permute-start.10 = (bf16[128,512]{1,0:T(8,128)(2,1)S(1)}, bf16[128,512]{1,0:T(8,128)(2,1)S(1)}, u32[]{:S(2)}, u32[]{:S(2)}) collective-permute-start(bf16[128,512]{1,0:T(8,128)(2,1)S(1)} %bitcast.92), channel_id=1, source_target_pairs={{64,0},{96,32},{128,64},{160,96},{192,128},{224,160},{0,192},{32,2... | collective-permute-start | bytes 393224 | tf_op jit(solution)/shard_map/ppermute | solution.py:23
  70.4 2.0 collective-permute-done.9
  72.4 2.3 %collective-permute-start.11 = (bf16[128,512]{1,0:T(8,128)(2,1)S(1)}, bf16[128,512]{1,0:T(8,128)(2,1)S(1)}, u32[]{:S(2)}, u32[]{:S(2)}) collective-permute-start(bf16[128,512]{1,0:T(8,128)(2,1)S(1)} %collective-permute-done.9), channel_id=1, source_target_pairs={{64,0},{96,32},{128,64},{160,96},{192,128},{224,160},{0,192},{32,2... | collective-permute-start | bytes 393224 | tf_op jit(solution)/shard_map/ppermute | solution.py:23
  75.9 4.8 %collective-permute-done.11 = bf16[128,512]{1,0:T(8,128)(2,1)S(1)} collective-permute-done((bf16[128,512]{1,0:T(8,128)(2,1)S(1)}, bf16[128,512]{1,0:T(8,128)(2,1)S(1)}, u32[]{:S(2)}, u32[]{:S(2)}) %collective-permute-start.11) | collective-permute-done | bytes 131104 | tf_op jit(solution)/shard_map/ppermute | solution.py:23
  80.8 2.8 %collective-permute-start.12 = (bf16[128,512]{1,0:T(8,128)(2,1)S(1)}, bf16[128,512]{1,0:T(8,128)(2,1)S(1)}, u32[]{:S(2)}, u32[]{:S(2)}) collective-permute-start(bf16[128,512]{1,0:T(8,128)(2,1)S(1)} %collective-permute-done.11), channel_id=1, source_target_pairs={{32,0},{64,32},{96,64},{128,96},{160,128},{192,160},{224,192},{0,2... | collective-permute-start | bytes 393224 | tf_op jit(solution)/shard_map/ppermute | solution.py:23
  83.6 2.5 %collective-permute-done.12 = bf16[128,512]{1,0:T(8,128)(2,1)S(1)} collective-permute-done((bf16[128,512]{1,0:T(8,128)(2,1)S(1)}, bf16[128,512]{1,0:T(8,128)(2,1)S(1)}, u32[]{:S(2)}, u32[]{:S(2)}) %collective-permute-start.12) | collective-permute-done | bytes 131104 | tf_op jit(solution)/shard_map/ppermute | solution.py:23
  87.3 30.0 %all_to_all.25 = bf16[8,32,4096]{2,1,0:T(8,128)(2,1)S(1)} all-to-all(bf16[8,32,4096]{2,1,0:T(8,128)(2,1)S(1)} %bitcast.81), channel_id=1, replica_groups=mesh['z'=8,'xl'=2,'xh'=2,'y'=4,'c'=2] {'xh','y'}, dimensions={0} | all-to-all | bytes 4194304 | tf_op jit(solution)/shard_map/all_to_all | solution.py:103
  118.6 4.2 %collective-permute-done.16 = bf16[256,4096]{1,0:T(8,128)(2,1)S(1)} collective-permute-done((bf16[256,4096]{1,0:T(8,128)(2,1)S(1)}, bf16[256,4096]{1,0:T(8,128)(2,1)S(1)}, u32[]{:S(2)}, u32[]{:S(2)}) %collective-permute-start.16) | collective-permute-done | bytes 2097184 | tf_op jit(solution)/shard_map/ppermute | solution.py:19
  124.2 2.1 fusion.6
  126.2 6.4 %convolution_convert_fusion.1 = bf16[256,4096]{1,0:T(8,128)(2,1)} fusion(bf16[1,384,4096]{2,1,0:T(8,128)(2,1)S(1)} %copy-done, f32[256,384]{1,0:T(8,128)} %fusion.6, bf16[256,4096]{1,0:T(8,128)(2,1)} %copy-done.6, bf16[1,4096,384]{2,1,0:T(8,128)(2,1)} %param.13), kind=kOutput, calls=%fused_computation.1 | convolution fusion | flops 1612251136 | bytes 10878976 | tf_op jit(solution)/shard_map/dot_general | solution.py:38
  132.7 4.5 %fusion.12 = f32[256,384]{1,0:T(8,128)} fusion(bf16[256,4096]{1,0:T(8,128)(2,1)} %bitcast.86, bf16[1,4096,384]{2,1,0:T(8,128)(2,1)} %param.13), kind=kOutput, calls=%fused_computation.14 | convolution fusion | flops 805306368 | bytes 5636096 | tf_op jit(solution)/shard_map/dot_general | solution.py:35
  137.3 7.1 %add_convert_fusion = bf16[256,4096]{1,0:T(8,128)(2,1)} fusion(bf16[256,4096]{1,0:T(8,128)(2,1)} %collective-permute-done.17, bf16[1,384,4096]{2,1,0:T(8,128)(2,1)S(1)} %copy-done, bf16[256,4096]{1,0:T(8,128)(2,1)} %bitcast.87, bf16[1,4096,384]{2,1,0:T(8,128)(2,1)} %param.14, f32[256,384]{1,0:T(8,128)} %fusion.12), kind=kOutput, calls=%fused_computation.4 | convolution fusion | flops 1614348288 | bytes 12976128 | tf_op jit(solution)/shard_map/dot_general | solution.py:38
  144.3 7.2 %all-to-all-start.3 = ((bf16[8,32,4096]{2,1,0:T(8,128)(2,1)}), bf16[8,32,4096]{2,1,0:T(8,128)(2,1)}, u32[]{:S(2)}, u32[]{:S(2)}) async-start(bf16[8,32,4096]{2,1,0:T(8,128)(2,1)} %bitcast.84), calls=%async_computation.3 | async-start | bytes 4194304 | tf_op jit(solution)/shard_map/all_to_all | solution.py:110
  151.7 26.2 %all-to-all-done.3 = bf16[8,32,4096]{2,1,0:T(8,128)(2,1)} async-done(((bf16[8,32,4096]{2,1,0:T(8,128)(2,1)}), bf16[8,32,4096]{2,1,0:T(8,128)(2,1)}, u32[]{:S(2)}, u32[]{:S(2)}) %all-to-all-start.3) | async-done | bytes 2097184 | tf_op jit(solution)/shard_map/all_to_all | solution.py:110
  177.9 2.1 fusion.52
  179.9 2.1 fusion
  185.3 12.5 %collective-permute-done.18 = bf16[8,8,4096]{2,1,0:T(8,128)(2,1)} collective-permute-done((bf16[8,8,4096]{2,1,0:T(8,128)(2,1)}, bf16[8,8,4096]{2,1,0:T(8,128)(2,1)}, u32[]{:S(2)}, u32[]{:S(2)}) %collective-permute-start.18) | collective-permute-done | bytes 524320 | tf_op jit(solution)/shard_map/ppermute | solution.py:19
  197.8 2.1 fusion.24
  200.0 7.3 %all-to-all-start.4 = ((bf16[8,8,4096]{2,1,0:T(8,128)(2,1)}), bf16[8,8,4096]{2,1,0:T(8,128)(2,1)}, u32[]{:S(2)}, u32[]{:S(2)}) async-start(bf16[8,8,4096]{2,1,0:T(8,128)(2,1)} %fusion.24), calls=%async_computation.4 | async-start | bytes 1048576 | tf_op jit(solution)/shard_map/all_to_all | solution.py:121
  207.3 17.0 %all-to-all-done.4 = bf16[8,8,4096]{2,1,0:T(8,128)(2,1)} async-done(((bf16[8,8,4096]{2,1,0:T(8,128)(2,1)}), bf16[8,8,4096]{2,1,0:T(8,128)(2,1)}, u32[]{:S(2)}, u32[]{:S(2)}) %all-to-all-start.4) | async-done | bytes 524320 | tf_op jit(solution)/shard_map/all_to_all | solution.py:121
  (91 shorter events, 23.6 us)
Async XLA Ops:
  0.0 126.2 %copy-start = (bf16[1,384,4096]{2,1,0:T(8,128)(2,1)S(1)}, bf16[1,384,4096]{2,1,0:T(8,128)(2,1)}, u32[]{:S(2)}) copy-start(bf16[1,384,4096]{2,1,0:T(8,128)(2,1)} %param.15) | copy-start | bytes 9437188
  0.0 20.0 %collective-permute-start = (bf16[128,512]{1,0:T(8,128)(2,1)}, bf16[128,512]{1,0:T(8,128)(2,1)}, u32[]{:S(2)}, u32[]{:S(2)}) collective-permute-start(bf16[128,512]{1,0:T(8,128)(2,1)} %param.8), channel_id=1, source_target_pairs={{32,0},{64,32},{96,64},{128,96},{160,128},{192,160},{224,192},{0,2... | collective-permute-start | bytes 393224 | tf_op jit(solution)/shard_map/ppermute | solution.py:23
  5.9 18.8 %collective-permute-start.1 = (bf16[128,512]{1,0:T(8,128)(2,1)}, bf16[128,512]{1,0:T(8,128)(2,1)}, u32[]{:S(2)}, u32[]{:S(2)}) collective-permute-start(bf16[128,512]{1,0:T(8,128)(2,1)} %param.8), channel_id=1, source_target_pairs={{64,0},{96,32},{128,64},{160,96},{192,128},{224,160},{0,192},{32,2... | collective-permute-start | bytes 393224 | tf_op jit(solution)/shard_map/ppermute | solution.py:23
  7.3 16.4 %collective-permute-start.4 = (bf16[128,512]{1,0:T(8,128)(2,1)}, bf16[128,512]{1,0:T(8,128)(2,1)S(1)}, u32[]{:S(2)}, u32[]{:S(2)}) collective-permute-start(bf16[128,512]{1,0:T(8,128)(2,1)} %param.8), channel_id=1, source_target_pairs={{224,0},{0,32},{32,64},{64,96},{96,128},{128,160},{160,192},{192,2... | collective-permute-start | bytes 393224 | tf_op jit(solution)/shard_map/ppermute | solution.py:23
  8.3 24.9 %collective-permute-start.6 = (bf16[128,512]{1,0:T(8,128)(2,1)}, bf16[128,512]{1,0:T(8,128)(2,1)S(1)}, u32[]{:S(2)}, u32[]{:S(2)}) collective-permute-start(bf16[128,512]{1,0:T(8,128)(2,1)} %param.8), channel_id=1, source_target_pairs={{192,0},{224,32},{0,64},{32,96},{64,128},{96,160},{128,192},{160,2... | collective-permute-start | bytes 393224 | tf_op jit(solution)/shard_map/ppermute | solution.py:23
  10.9 24.1 %all-to-all-start.1 = ((f32[16,1,128]{2,1,0:T(1,128)}), f32[16,1,128]{2,1,0:T(1,128)S(1)}, u32[]{:S(2)}, u32[]{:S(2)}) async-start(f32[16,1,128]{2,1,0:T(1,128)} %reshape.201), calls=%async_computation.1 | async-start | bytes 16384 | tf_op jit(solution)/shard_map/all_to_all | solution.py:53
  17.1 16.2 %copy-start.7 = (bf16[512,256]{1,0:T(8,128)(2,1)S(1)}, bf16[512,256]{1,0:T(8,128)(2,1)}, u32[]{:S(2)}) copy-start(bf16[512,256]{1,0:T(8,128)(2,1)} %param.9) | copy-start | bytes 786436
  17.1 16.2 %collective-permute-start.7 = (bf16[512,256]{1,0:T(8,128)(2,1)}, bf16[512,256]{1,0:T(8,128)(2,1)S(1)}, u32[]{:S(2)}, u32[]{:S(2)}) collective-permute-start(bf16[512,256]{1,0:T(8,128)(2,1)} %param.9), channel_id=1, source_target_pairs={{0,16},{16,0},{1,17},{17,1},{2,18},{18,2},{3,19},{19,3},{4,20},{20... | collective-permute-start | bytes 786440 | tf_op jit(solution)/shard_map/ppermute | solution.py:19
  20.0 7.9 %collective-permute-start.2 = (bf16[128,512]{1,0:T(8,128)(2,1)}, bf16[128,512]{1,0:T(8,128)(2,1)S(1)}, u32[]{:S(2)}, u32[]{:S(2)}) collective-permute-start(bf16[128,512]{1,0:T(8,128)(2,1)} %collective-permute-done), channel_id=1, source_target_pairs={{64,0},{96,32},{128,64},{160,96},{192,128},{224,160},{0,192},{32,2... | collective-permute-start | bytes 393224 | tf_op jit(solution)/shard_map/ppermute | solution.py:23
  23.7 9.5 %collective-permute-start.5 = (bf16[128,512]{1,0:T(8,128)(2,1)S(1)}, bf16[128,512]{1,0:T(8,128)(2,1)S(1)}, u32[]{:S(2)}, u32[]{:S(2)}) collective-permute-start(bf16[128,512]{1,0:T(8,128)(2,1)S(1)} %collective-permute-done.4), channel_id=1, source_target_pairs={{192,0},{224,32},{0,64},{32,96},{64,128},{96,160},{128,192},{160,2... | collective-permute-start | bytes 393224 | tf_op jit(solution)/shard_map/ppermute | solution.py:23
  27.9 5.3 %collective-permute-start.3 = (bf16[128,512]{1,0:T(8,128)(2,1)S(1)}, bf16[128,512]{1,0:T(8,128)(2,1)S(1)}, u32[]{:S(2)}, u32[]{:S(2)}) collective-permute-start(bf16[128,512]{1,0:T(8,128)(2,1)S(1)} %collective-permute-done.2), channel_id=1, source_target_pairs={{32,0},{64,32},{96,64},{128,96},{160,128},{192,160},{224,192},{0,2... | collective-permute-start | bytes 393224 | tf_op jit(solution)/shard_map/ppermute | solution.py:23
  35.0 22.8 %all-to-all-start = ((bf16[16,64,512]{2,1,0:T(8,128)(2,1)}), bf16[16,64,512]{2,1,0:T(8,128)(2,1)}, u32[]{:S(2)}, u32[]{:S(2)}) async-start(bf16[16,64,512]{2,1,0:T(8,128)(2,1)} %bitcast.88), calls=%async_computation | async-start | bytes 2097152 | tf_op jit(solution)/shard_map/all_to_all | solution.py:61
  59.2 4.4 %collective-permute-start.8 = (bf16[64,512]{1,0:T(8,128)(2,1)S(1)}, bf16[64,512]{1,0:T(8,128)(2,1)S(1)}, u32[]{:S(2)}, u32[]{:S(2)}) collective-permute-start(bf16[64,512]{1,0:T(8,128)(2,1)S(1)} %maximum_select_fusion.2), channel_id=1, source_target_pairs={{0,16},{16,0},{1,17},{17,1},{2,18},{18,2},{3,19},{19,3},{4,20},{20... | collective-permute-start | bytes 196616 | tf_op jit(solution)/shard_map/ppermute | solution.py:19
  63.7 8.8 %collective-permute-start.9 = (bf16[128,512]{1,0:T(8,128)(2,1)S(1)}, bf16[128,512]{1,0:T(8,128)(2,1)S(1)}, u32[]{:S(2)}, u32[]{:S(2)}) collective-permute-start(bf16[128,512]{1,0:T(8,128)(2,1)S(1)} %bitcast.90), channel_id=1, source_target_pairs={{32,0},{64,32},{96,64},{128,96},{160,128},{192,160},{224,192},{0,2... | collective-permute-start | bytes 393224 | tf_op jit(solution)/shard_map/ppermute | solution.py:23
  67.4 8.5 %collective-permute-start.13 = (bf16[128,512]{1,0:T(8,128)(2,1)S(1)}, bf16[128,512]{1,0:T(8,128)(2,1)S(1)}, u32[]{:S(2)}, u32[]{:S(2)}) collective-permute-start(bf16[128,512]{1,0:T(8,128)(2,1)S(1)} %bitcast.91), channel_id=1, source_target_pairs={{224,0},{0,32},{32,64},{64,96},{96,128},{128,160},{160,192},{192,2... | collective-permute-start | bytes 393224 | tf_op jit(solution)/shard_map/ppermute | solution.py:23
  67.4 19.1 %copy-start.4 = (f32[4096]{0:T(1024)S(1)}, f32[4096]{0:T(1024)}, u32[]{:S(2)}) copy-start(f32[4096]{0:T(1024)} %param.10) | copy-start | bytes 49156
  67.4 16.1 %collective-permute-start.10 = (bf16[128,512]{1,0:T(8,128)(2,1)S(1)}, bf16[128,512]{1,0:T(8,128)(2,1)S(1)}, u32[]{:S(2)}, u32[]{:S(2)}) collective-permute-start(bf16[128,512]{1,0:T(8,128)(2,1)S(1)} %bitcast.92), channel_id=1, source_target_pairs={{64,0},{96,32},{128,64},{160,96},{192,128},{224,160},{0,192},{32,2... | collective-permute-start | bytes 393224 | tf_op jit(solution)/shard_map/ppermute | solution.py:23
  70.1 16.0 %collective-permute-start.15 = (bf16[128,512]{1,0:T(8,128)(2,1)S(1)}, bf16[128,512]{1,0:T(8,128)(2,1)S(1)}, u32[]{:S(2)}, u32[]{:S(2)}) collective-permute-start(bf16[128,512]{1,0:T(8,128)(2,1)S(1)} %bitcast.93), channel_id=1, source_target_pairs={{192,0},{224,32},{0,64},{32,96},{64,128},{96,160},{128,192},{160,2... | collective-permute-start | bytes 393224 | tf_op jit(solution)/shard_map/ppermute | solution.py:23
  72.4 8.4 %collective-permute-start.11 = (bf16[128,512]{1,0:T(8,128)(2,1)S(1)}, bf16[128,512]{1,0:T(8,128)(2,1)S(1)}, u32[]{:S(2)}, u32[]{:S(2)}) collective-permute-start(bf16[128,512]{1,0:T(8,128)(2,1)S(1)} %collective-permute-done.9), channel_id=1, source_target_pairs={{64,0},{96,32},{128,64},{160,96},{192,128},{224,160},{0,192},{32,2... | collective-permute-start | bytes 393224 | tf_op jit(solution)/shard_map/ppermute | solution.py:23
  75.9 10.2 %collective-permute-start.14 = (bf16[128,512]{1,0:T(8,128)(2,1)S(1)}, bf16[128,512]{1,0:T(8,128)(2,1)S(1)}, u32[]{:S(2)}, u32[]{:S(2)}) collective-permute-start(bf16[128,512]{1,0:T(8,128)(2,1)S(1)} %collective-permute-done.13), channel_id=1, source_target_pairs={{192,0},{224,32},{0,64},{32,96},{64,128},{96,160},{128,192},{160,2... | collective-permute-start | bytes 393224 | tf_op jit(solution)/shard_map/ppermute | solution.py:23
  80.8 5.3 %collective-permute-start.12 = (bf16[128,512]{1,0:T(8,128)(2,1)S(1)}, bf16[128,512]{1,0:T(8,128)(2,1)S(1)}, u32[]{:S(2)}, u32[]{:S(2)}) collective-permute-start(bf16[128,512]{1,0:T(8,128)(2,1)S(1)} %collective-permute-done.11), channel_id=1, source_target_pairs={{32,0},{64,32},{96,64},{128,96},{160,128},{192,160},{224,192},{0,2... | collective-permute-start | bytes 393224 | tf_op jit(solution)/shard_map/ppermute | solution.py:23
  86.2 1.1 copy-start.1
  87.3 36.8 %copy-start.5 = (bf16[1,4096,384]{2,1,0:T(8,128)(2,1)S(1)}, bf16[1,4096,384]{2,1,0:T(8,128)(2,1)}, u32[]{:S(2)}) copy-start(bf16[1,4096,384]{2,1,0:T(8,128)(2,1)} %param.14) | copy-start | bytes 9437188
  117.3 1.3 copy-start.3
  118.6 4.2 %collective-permute-start.16 = (bf16[256,4096]{1,0:T(8,128)(2,1)S(1)}, bf16[256,4096]{1,0:T(8,128)(2,1)S(1)}, u32[]{:S(2)}, u32[]{:S(2)}) collective-permute-start(bf16[256,4096]{1,0:T(8,128)(2,1)S(1)} %bitcast.85), channel_id=1, source_target_pairs={{0,1},{1,0},{2,3},{3,2},{4,5},{5,4},{6,7},{7,6},{8,9},{9,8},{10,11... | collective-permute-start | bytes 6291464 | tf_op jit(solution)/shard_map/ppermute | solution.py:19
  122.8 1.4 copy-start.6
  132.6 4.7 %collective-permute-start.17 = (bf16[256,4096]{1,0:T(8,128)(2,1)}, bf16[256,4096]{1,0:T(8,128)(2,1)}, u32[]{:S(2)}, u32[]{:S(2)}) collective-permute-start(bf16[256,4096]{1,0:T(8,128)(2,1)} %convolution_convert_fusion.1), channel_id=1, source_target_pairs={{0,1},{1,0},{2,3},{3,2},{4,5},{5,4},{6,7},{7,6},{8,9},{9,8},{10,11... | collective-permute-start | bytes 6291464 | tf_op jit(solution)/shard_map/ppermute | solution.py:19
  144.3 33.6 %all-to-all-start.3 = ((bf16[8,32,4096]{2,1,0:T(8,128)(2,1)}), bf16[8,32,4096]{2,1,0:T(8,128)(2,1)}, u32[]{:S(2)}, u32[]{:S(2)}) async-start(bf16[8,32,4096]{2,1,0:T(8,128)(2,1)} %bitcast.84), calls=%async_computation.3 | async-start | bytes 4194304 | tf_op jit(solution)/shard_map/all_to_all | solution.py:110
  182.1 1.0 copy-start.2
  183.9 13.9 %collective-permute-start.18 = (bf16[8,8,4096]{2,1,0:T(8,128)(2,1)}, bf16[8,8,4096]{2,1,0:T(8,128)(2,1)}, u32[]{:S(2)}, u32[]{:S(2)}) collective-permute-start(bf16[8,8,4096]{2,1,0:T(8,128)(2,1)} %dynamic-slice_bitcast_fusion), channel_id=1, source_target_pairs={{0,16},{16,0},{1,17},{17,1},{2,18},{18,2},{3,19},{19,3},{4,20},{20... | collective-permute-start | bytes 1572872 | tf_op jit(solution)/shard_map/ppermute | solution.py:19
  200.0 24.3 %all-to-all-start.4 = ((bf16[8,8,4096]{2,1,0:T(8,128)(2,1)}), bf16[8,8,4096]{2,1,0:T(8,128)(2,1)}, u32[]{:S(2)}, u32[]{:S(2)}) async-start(bf16[8,8,4096]{2,1,0:T(8,128)(2,1)} %fusion.24), calls=%async_computation.4 | async-start | bytes 1048576 | tf_op jit(solution)/shard_map/all_to_all | solution.py:121
